TPU v7x, 32 devices: a whole 2x2x4 slice. The times are simulated.
32 devices in a mesh: groups: 2 (over y), date: 4 (over z), pix: 2 (over x), chan: 2 (over core).
Axes of the slice: x: 2, y: 2, z: 4, core: 2. Of those that a mesh axis runs over, the one named last changes fastest.
Arguments:
- frames: bfloat16 [128, 4, 64, 128], P(('groups', 'date'), 'pix'), parts along dimension 0, may hold values from -6 to 6
- spatial_weight: bfloat16 [3, 3, 64, 64], P(None, None, None, 'chan'), may hold values from -0.25 to 0.25
- spatial_bias: float32 [64], P('chan'), may hold values from -3 to 3
- temporal_weight: bfloat16 [64, 64, 16], P('date', 'chan'), may hold values from -0.1875 to 0.1875
- temporal_bias: float32 [16], replicated, may hold values from -4 to 4
- head_weight: float32 [16], replicated, may hold values from -3 to 3
- labels: int32 [8, 128], P(('groups', 'pix'), ('date', 'chan')), parts along dimension 0, may hold values 0 or 1
Outputs:
- logits: float32 [8, 128], P(('groups', 'pix'), ('date', 'chan')), parts along dimension 0
- grad_spatial: float32 [6, 3, 64, 64], P('groups', None, None, 'chan'), parts along dimension 0
- grad_temporal: float32 [64, 64, 32], P('date', 'chan', 'groups'), parts along dimension 2
There are 2 independent parts, one for each index of `groups`. A program takes and returns all parts, laid end to end along the dimension named above; an argument that names none is the same for every part. Nothing has to cross between parts.
All inputs are finite; a program needn't handle non-finite values. No bound on the sum of `labels` on one device may be relied on, other than what follows from the above.
Results may differ from a plain program's by a relative error of at most 0.024.
Values may be sent and summed in bfloat16 or wider, within the bound.
A program may use at most 64 MiB of HBM per device.

v0:
```python
import jax
import jax.numpy as jnp
from jax import lax
from jax.sharding import PartitionSpec as P


def with_halo(block, sides, width):
    for axis, dim in sides:
        count = lax.axis_size(axis)
        forward = [(i, i + 1) for i in range(count - 1)]
        backward = [(target, source) for source, target in forward]
        low = lax.ppermute(
            lax.slice_in_dim(block, block.shape[dim] - width, None, axis=dim), axis, forward
        )
        high = lax.ppermute(lax.slice_in_dim(block, 0, width, axis=dim), axis, backward)
        block = jnp.concatenate([low, block, high], axis=dim)
    return block


def shards(
    frames, spatial_weight, spatial_bias, temporal_weight, temporal_bias, head_weight, labels
):
    dates_here, rows, channels, columns = frames.shape
    padded = with_halo(frames, (("pix", 1),), 1)
    padded = jnp.pad(padded, ((0, 0), (0, 0), (0, 0), (1, 1)))
    preact = spatial_bias[None, None, :, None]
    for row_off in range(3):
        for col_off in range(3):
            window = padded[:, row_off : row_off + rows, :, col_off : col_off + columns]
            preact = preact + jnp.einsum(
                "ticj,co->tioj",
                window,
                spatial_weight[row_off, col_off],
                preferred_element_type=jnp.float32,
            )
    sigmoid_pre = jax.nn.sigmoid(preact)
    hidden = (preact * sigmoid_pre).astype(jnp.bfloat16)
    partial_feat = jnp.einsum(
        "tioj,tof->fij", hidden, temporal_weight, preferred_element_type=jnp.float32
    )
    feature = (
        lax.psum_scatter(partial_feat, ("date", "chan"), scatter_dimension=2, tiled=True)
        + temporal_bias[:, None, None]
    )
    sigmoid_feat = jax.nn.sigmoid(feature)
    logits = jnp.einsum("fij,f->ij", feature * sigmoid_feat, head_weight)
    dlogit = jax.nn.sigmoid(logits) - labels.astype(jnp.float32)
    feature_grad = (
        dlogit[None]
        * head_weight[:, None, None]
        * sigmoid_feat
        * (1.0 + feature * (1.0 - sigmoid_feat))
    ).astype(jnp.bfloat16)
    full_grad = lax.all_gather(feature_grad, ("date", "chan"), axis=2, tiled=True)
    temporal_part = jnp.einsum(
        "tioj,fij->tof", hidden, full_grad, preferred_element_type=jnp.float32
    )
    hidden_grad = jnp.einsum(
        "fij,tof->tioj", full_grad, temporal_weight, preferred_element_type=jnp.float32
    )
    preact_grad = (hidden_grad * sigmoid_pre * (1.0 + preact * (1.0 - sigmoid_pre))).astype(
        jnp.bfloat16
    )
    rows_out = []
    for row_off in range(3):
        cols_out = []
        for col_off in range(3):
            window = padded[:, row_off : row_off + rows, :, col_off : col_off + columns]
            cols_out.append(
                jnp.einsum("ticj,tioj->co", window, preact_grad, preferred_element_type=jnp.float32)
            )
        rows_out.append(jnp.stack(cols_out))
    spatial_part = jnp.stack(rows_out)
    grad_temporal = lax.psum(temporal_part, "pix")
    grad_spatial = lax.psum(spatial_part, ("date", "pix"))
    return (logits, grad_spatial, grad_temporal)


def solution(mesh):
    placed = (
        P(("groups", "date"), "pix", None, None),
        P(None, None, None, "chan"),
        P("chan"),
        P("date", "chan", None),
        P(),
        P(),
        P(("groups", "pix"), ("date", "chan")),
    )
    return jax.shard_map(
        shards,
        mesh=mesh,
        in_specs=placed,
        out_specs=(
            P(("groups", "pix"), ("date", "chan")),
            P("groups", None, None, "chan"),
            P("date", "chan", "groups"),
        ),
        check_vma=False,
    )
```

profile of v0, /device:TPU:0, one launch (start us, length us, event | category | flops | bytes accessed | tf_op | source)
XLA Modules:
  0.0 157.4 jit_solution(17748076628413484052)
XLA Ops:
  7.2 1.1 fusion.79
  8.4 4.9 %collective-permute-start = (bf16[16,1,64,128]{3,2,1,0:T(8,128)(2,1)S(1)}, bf16[16,1,64,128]{3,2,1,0:T(8,128)(2,1)S(1)}, u32[]{:S(2)}, u32[]{:S(2)}) collective-permute-start(bf16[16,1,64,128]{3,2,1,0:T(8,128)(2,1)S(1)} %get-tuple-element.11), channel_id=1, source_target_pairs={{0,2},{1,3},{4,6},{5,7},{8,10},{9,11},{12,14},{13,15},{16,18},{17,... | collective-permute-start | bytes 786440 | tf_op jit(solution)/shard_map/ppermute | solution.py:12
  13.3 1.4 collective-permute-start.1
  14.7 1.3 fusion.47
  16.0 2.8 %collective-permute-done = bf16[16,1,64,128]{3,2,1,0:T(8,128)(2,1)S(1)} collective-permute-done((bf16[16,1,64,128]{3,2,1,0:T(8,128)(2,1)S(1)}, bf16[16,1,64,128]{3,2,1,0:T(8,128)(2,1)S(1)}, u32[]{:S(2)}, u32[]{:S(2)}) %collective-permute-start) | collective-permute-done | bytes 262176 | tf_op jit(solution)/shard_map/ppermute | solution.py:12
  18.8 4.3 %collective-permute-done.1 = bf16[16,1,64,128]{3,2,1,0:T(8,128)(2,1)S(1)} collective-permute-done((bf16[16,1,64,128]{3,2,1,0:T(8,128)(2,1)S(1)}, bf16[16,1,64,128]{3,2,1,0:T(8,128)(2,1)S(1)}, u32[]{:S(2)}, u32[]{:S(2)}) %collective-permute-start.1) | collective-permute-done | bytes 262176 | tf_op jit(solution)/shard_map/ppermute | solution.py:15
  23.0 1.1 fusion.5
  24.2 0.4 fusion.40
  24.5 0.4 fusion.51
  26.0 0.2 fusion.15
  26.2 1.2 multiply_convert_fusion
  27.6 0.8 copy.76
  28.4 1.7 %reshape.35 = f32[128,32]{1,0:T(8,128)} reshape(f32[128,2,16]{2,1,0:T(2,128)} %bitcast.179) | data formatting | bytes 32768
  30.2 2.2 %fusion.78 = (bf16[16,2,64,128]{3,2,1,0:T(8,128)(2,1)}, bf16[16,2,64,128]{3,2,1,0:T(8,128)(2,1)}, bf16[16,2,64,128]{3,2,1,0:T(8,128)(2,1)}, bf16[16,2,64,128]{3,...) fusion(bf16[16,4,64,130]{3,2,1,0:T(8,128)(2,1)S(1)} %fusion.5), kind=kLoop, calls=%fused_computation.104 | loop fusion | bytes 6291456 | tf_op jit(solution)/shard_map/slice | solution.py:29
  32.4 28.2 %reduce-scatter.4.cloned.1.call-done = f32[16,32]{1,0:T(8,128)} async-done(((f32[128,32]{1,0:T(8,128)}), f32[16,32]{1,0:T(8,128)}) %reduce-scatter.4.cloned.1.call-update) | async-done | bytes 2064
  60.6 0.8 reshape.36
  61.9 14.0 %all_gather.3 = bf16[16,2,128]{0,1,2:T(2,128)(2,1)S(1)} all-gather(bf16[16,2,16]{0,1,2:T(2,128)(2,1)S(1)} %copy.31), channel_id=1, replica_groups=mesh['groups'=2,'date'=4,'pix'=2,'chan'=2] {'date','chan'}, dimensions={2}, use_global_device_ids=true | all-gather | bytes 9216 | tf_op jit(solution)/shard_map/all_gather | solution.py:54
  75.9 1.4 fusion.16
  77.3 0.3 convolution_bitcast_fusion.10
  77.6 0.3 convolution_bitcast_fusion.4
  77.9 0.3 convolution_bitcast_fusion.7
  78.4 0.3 convolution_bitcast_fusion.11
  78.6 0.3 convolution_bitcast_fusion.5
  78.9 0.3 convolution_bitcast_fusion.6
  79.2 0.3 convolution_bitcast_fusion.8
  79.4 0.3 convolution_bitcast_fusion.9
  79.8 0.3 convolution_bitcast_fusion.3
  80.1 0.7 pad_maximum_fusion.2
  80.8 0.3 convolution_bitcast_fusion.1
  81.0 10.8 %psum.15 = f32[16,32,16]{1,2,0:T(8,128)} all-reduce(f32[16,32,16]{1,2,0:T(8,128)S(1)} %convolution_bitcast_fusion.1), channel_id=1, replica_groups=mesh['groups'=2,'date'=4,'pix'=2,'chan'=2] {'pix'}, use_global_device_ids=true, to_apply=%region_2.3 | all-reduce | flops 8192 | bytes 65536 | tf_op jit(solution)/shard_map/psum | solution.py:74
  91.8 57.2 %all-reduce.3.cloned.1.call-done = f32[3,3,64,32]{2,3,1,0:T(8,128)} async-done(((f32[3,3,64,32]{2,3,1,0:T(8,128)}), f32[3,3,64,32]{2,3,1,0:T(8,128)}) %all-reduce.3.cloned.1.call-update) | async-done | bytes 73744 | tf_op jit(solution)/shard_map/psum | solution.py:75
  149.0 1.6 %copy.115 = f32[3,3,64,32]{2,3,1,0:T(8,128)} copy(f32[3,3,64,32]{2,3,1,0:T(8,128)} %all-reduce.3.cloned.1.call-done) | data formatting | bytes 147456
  (50 shorter events, 2.3 us)
Async XLA Ops:
  7.2 20.3 %copy-start = (bf16[16,32,16]{1,2,0:T(8,128)(2,1)S(1)}, bf16[16,32,16]{1,2,0:T(8,128)(2,1)}, u32[]{:S(2)}) copy-start(bf16[16,32,16]{1,2,0:T(8,128)(2,1)} %param.10) | copy-start | bytes 49156
  7.2 15.9 %copy-start.1 = (bf16[16,2,64,128]{3,2,1,0:T(8,128)(2,1)S(1)}, bf16[16,2,64,128]{3,2,1,0:T(8,128)(2,1)}, u32[]{:S(2)}) copy-start(bf16[16,2,64,128]{3,2,1,0:T(8,128)(2,1)} %param.7) | copy-start | bytes 1572868
  7.2 53.4 %reduce-scatter.4.cloned.1.call-start = ((), (), s32[]{:S(2)}) async-start(), calls=%async_computation.2 | async-start | bytes 73728
  8.4 10.4 %collective-permute-start = (bf16[16,1,64,128]{3,2,1,0:T(8,128)(2,1)S(1)}, bf16[16,1,64,128]{3,2,1,0:T(8,128)(2,1)S(1)}, u32[]{:S(2)}, u32[]{:S(2)}) collective-permute-start(bf16[16,1,64,128]{3,2,1,0:T(8,128)(2,1)S(1)} %get-tuple-element.11), channel_id=1, source_target_pairs={{0,2},{1,3},{4,6},{5,7},{8,10},{9,11},{12,14},{13,15},{16,18},{17,... | collective-permute-start | bytes 786440 | tf_op jit(solution)/shard_map/ppermute | solution.py:12
  13.2 10.9 %copy-start.10 = (bf16[3,3,64,32]{2,3,1,0:T(8,128)(2,1)S(1)}, bf16[3,3,64,32]{2,3,1,0:T(8,128)(2,1)}, u32[]{:S(2)}) copy-start(bf16[3,3,64,32]{2,3,1,0:T(8,128)(2,1)} %param.8) | copy-start | bytes 110596
  13.3 9.8 %collective-permute-start.1 = (bf16[16,1,64,128]{3,2,1,0:T(8,128)(2,1)S(1)}, bf16[16,1,64,128]{3,2,1,0:T(8,128)(2,1)S(1)}, u32[]{:S(2)}, u32[]{:S(2)}) collective-permute-start(bf16[16,1,64,128]{3,2,1,0:T(8,128)(2,1)S(1)} %get-tuple-element.12), channel_id=1, source_target_pairs={{2,0},{3,1},{6,4},{7,5},{10,8},{11,9},{14,12},{15,13},{18,16},{19,... | collective-permute-start | bytes 786440 | tf_op jit(solution)/shard_map/ppermute | solution.py:15
  25.3 0.7 copy-start.15
  25.4 0.8 copy-start.2
  30.1 31.4 %copy-start.13 = (f32[16]{0:T(128)S(1)}, f32[16]{0:T(128)}, u32[]{:S(2)}) copy-start(f32[16]{0:T(128)} %param.11) | copy-start | bytes 196
  30.1 31.4 %copy-start.14 = (f32[16]{0:T(128)S(1)}, f32[16]{0:T(128)}, u32[]{:S(2)}) copy-start(f32[16]{0:T(128)} %param.12) | copy-start | bytes 196
  30.1 31.5 %copy-start.11 = (s32[2,16]{1,0:T(2,128)S(1)}, s32[2,16]{1,0:T(2,128)}, u32[]{:S(2)}) copy-start(s32[2,16]{1,0:T(2,128)} %param.13) | copy-start | bytes 388
  30.1 118.9 %all-reduce.3.cloned.1.call-start = ((), (), s32[]{:S(2)}) async-start(), calls=%async_computation.1 | async-start | bytes 294912 | tf_op jit(solution)/shard_map/psum | solution.py:75
  32.4 44.9 %copy-start.3 = (bf16[16,2,64,128]{3,2,1,0:T(8,128)(2,1)S(1)}, bf16[16,2,64,128]{3,2,1,0:T(8,128)(2,1)}, u32[]{:S(2)}) copy-start(bf16[16,2,64,128]{3,2,1,0:T(8,128)(2,1)} %copy-done.2) | copy-start | bytes 1572868
  61.6 16.2 %copy-start.12 = (f32[1,2,16]{2,0,1:T(1,128)}, f32[1,2,16]{2,0,1:T(1,128)S(1)}, u32[]{:S(2)}) copy-start(f32[1,2,16]{2,0,1:T(1,128)S(1)} %fusion.28) | copy-start | bytes 388
  77.3 1.0 copy-start.9
  77.3 1.3 copy-start.8
  77.6 1.3 copy-start.7
  77.9 1.3 copy-start.6
  78.1 1.3 copy-start.5
  78.6 1.2 copy-start.4
Sparse Core Ops, SparseCore 0:
  30.2 30.3 reduce-scatter.3
  80.9 68.0 all-reduce.2
where the time goes:
time: 158 us; the launch traced here: 157 us
  waiting for transfers between devices  92.5 us (59%)
  blocking collectives  24.7 us (16%)
  between operations  14.3 us (9%)
  local copies, waits for them, and re-layouts  8.89 us (6%)
  matrix products  8.7 us (6%)
  starting transfers between devices  6.36 us (4%)
  other arithmetic  1.98 us (1%)
    psum x1, waiting for transfers between devices, shards(): grad_spatial = lax.psum(spatial_part, ('date', 'pix'))  57.2 us
    unnamed x3, waiting for transfers between devices  28.2 us
    all_gather x1, blocking collectives, shards(): lax.all_gather(feature_grad, ('date', 'chan'), axis=2, tiled=True)  14 us
    psum x1, blocking collectives, shards(): grad_temporal = lax.psum(temporal_part, 'pix')  10.8 us
    unnamed x37, local copies, waits for them, and re-layouts  5.36 us
    ppermute x1, starting transfers between devices, with_halo(): lax.ppermute(lax.slice_in_dim(block, block.shape[dim] - width, None, axis...  4.86 us
    ppermute x1, waiting for transfers between devices, with_halo(): lax.ppermute(lax.slice_in_dim(block, 0, width, axis=dim), axis, backward)  4.27 us
    dot_general x9, matrix products, shards(): jnp.einsum('ticj,co->tioj', window, spatial_weight[row_off, col_off], pre...  4.27 us
  transfers between devices with their start and end apart: 4, of which 4 were waited for; matrix products, arithmetic and copies ran while one was open for 2% of the time, Pallas kernels for 0%

commit v1 on v0

--- a/solution.py
+++ b/solution.py
@@ -51,7 +51,18 @@
         * sigmoid_feat
         * (1.0 + feature * (1.0 - sigmoid_feat))
     ).astype(jnp.bfloat16)
-    full_grad = lax.all_gather(feature_grad, ("date", "chan"), axis=2, tiled=True)
+    ways = lax.axis_size(("date", "chan"))
+    up = [(d, (d + 1) % ways) for d in range(ways)]
+    down = [(d, (d - 1) % ways) for d in range(ways)]
+    earlier, later = ([feature_grad], [feature_grad])
+    for _ in range(ways // 2):
+        earlier.append(lax.ppermute(earlier[-1], ("date", "chan"), up))
+    for _ in range((ways - 1) // 2):
+        later.append(lax.ppermute(later[-1], ("date", "chan"), down))
+    line = jnp.concatenate([*earlier[::-1], *later[1:]], axis=2)
+    full_grad = jnp.roll(
+        line, (lax.axis_index(("date", "chan")) - ways // 2) * feature_grad.shape[2], axis=2
+    )
     temporal_part = jnp.einsum(
         "tioj,fij->tof", hidden, full_grad, preferred_element_type=jnp.float32
     )

time: 158 us -> 164 us (1.038)
  blocking collectives: 24.7 us -> 10.2 us
  starting transfers between devices: 6.36 us -> 17 us
  waiting for transfers between devices: 92.5 us -> 102 us
    all_gather x1 -> x0, blocking collectives: 14 us -> none  [shards(): lax.all_gather(feature_grad, ('date', 'chan'), axis=2, tiled=True)]
    ppermute x0 -> x7, starting transfers between devices: none -> 10.7 us  [the longest x3 10.6 us: shards(): later.append(lax.ppermute(later[-1], ('date', 'chan'), down))]
    ppermute x0 -> x7, waiting for transfers between devices: none -> 6.62 us  [the longest x4 6.49 us: shards(): earlier.append(lax.ppermute(earlier[-1], ('date', 'chan'), up))]
    unnamed x3, waiting for transfers between devices: 28.2 us -> 30.5 us
  transfers between devices with their start and end apart: 4 -> 11, of which waited for: 4 -> 9; matrix products, arithmetic and copies ran while one was open for 2% -> 2% of each run, Pallas kernels for 0% -> 0%
where the time goes in v1:
time: 164 us; the launch traced here: 163 us
  waiting for transfers between devices  102 us (62%)
  starting transfers between devices  17 us (10%)
  between operations  14.3 us (9%)
  blocking collectives  10.2 us (6%)
  local copies, waits for them, and re-layouts  8.86 us (5%)
  matrix products  8.78 us (5%)
  other arithmetic  1.98 us (1%)
    psum x1, waiting for transfers between devices, shards(): grad_spatial = lax.psum(spatial_part, ('date', 'pix'))  58 us
    unnamed x3, waiting for transfers between devices  30.5 us
    ppermute x3, starting transfers between devices, shards(): later.append(lax.ppermute(later[-1], ('date', 'chan'), down))  10.6 us
    psum x1, blocking collectives, shards(): grad_temporal = lax.psum(temporal_part, 'pix')  10.2 us
    ppermute x4, waiting for transfers between devices, shards(): earlier.append(lax.ppermute(earlier[-1], ('date', 'chan'), up))  6.49 us
    unnamed x37, local copies, waits for them, and re-layouts  5.37 us
    ppermute x1, starting transfers between devices, with_halo(): lax.ppermute(lax.slice_in_dim(block, block.shape[dim] - width, None, axis...  4.86 us
    dot_general x9, matrix products, shards(): jnp.einsum('ticj,co->tioj', window, spatial_weight[row_off, col_off], pre...  4.29 us
  transfers between devices with their start and end apart: 11, of which 9 were waited for; matrix products, arithmetic and copies ran while one was open for 2% of the time, Pallas kernels for 0%

profile of v1, /device:TPU:0, one launch (start us, length us, event | category | flops | bytes accessed | tf_op | source)
XLA Modules:
  0.0 163.3 jit_solution(16796424278508233526)
XLA Ops:
  7.2 1.1 fusion.83
  8.4 4.9 %collective-permute-start = (bf16[16,1,64,128]{3,2,1,0:T(8,128)(2,1)S(1)}, bf16[16,1,64,128]{3,2,1,0:T(8,128)(2,1)S(1)}, u32[]{:S(2)}, u32[]{:S(2)}) collective-permute-start(bf16[16,1,64,128]{3,2,1,0:T(8,128)(2,1)S(1)} %get-tuple-element.11), channel_id=1, source_target_pairs={{0,2},{1,3},{4,6},{5,7},{8,10},{9,11},{12,14},{13,15},{16,18},{17,... | collective-permute-start | bytes 786440 | tf_op jit(solution)/shard_map/ppermute | solution.py:12
  13.3 1.4 collective-permute-start.1
  14.7 1.3 fusion.47
  16.0 2.8 %collective-permute-done = bf16[16,1,64,128]{3,2,1,0:T(8,128)(2,1)S(1)} collective-permute-done((bf16[16,1,64,128]{3,2,1,0:T(8,128)(2,1)S(1)}, bf16[16,1,64,128]{3,2,1,0:T(8,128)(2,1)S(1)}, u32[]{:S(2)}, u32[]{:S(2)}) %collective-permute-start) | collective-permute-done | bytes 262176 | tf_op jit(solution)/shard_map/ppermute | solution.py:12
  18.8 4.3 %collective-permute-done.1 = bf16[16,1,64,128]{3,2,1,0:T(8,128)(2,1)S(1)} collective-permute-done((bf16[16,1,64,128]{3,2,1,0:T(8,128)(2,1)S(1)}, bf16[16,1,64,128]{3,2,1,0:T(8,128)(2,1)S(1)}, u32[]{:S(2)}, u32[]{:S(2)}) %collective-permute-start.1) | collective-permute-done | bytes 262176 | tf_op jit(solution)/shard_map/ppermute | solution.py:15
  23.0 1.1 fusion.5
  24.2 0.4 fusion.40
  24.5 0.4 fusion.51
  26.3 1.2 multiply_convert_fusion
  27.7 0.8 copy.73
  28.4 1.7 %reshape.34 = f32[128,32]{1,0:T(8,128)} reshape(f32[128,2,16]{2,1,0:T(2,128)} %bitcast.178) | data formatting | bytes 32768
  30.2 30.5 %reduce-scatter.4.cloned.1.call-done = f32[16,32]{1,0:T(8,128)} async-done(((f32[128,32]{1,0:T(8,128)}), f32[16,32]{1,0:T(8,128)}) %reduce-scatter.4.cloned.1.call-update) | async-done | bytes 2064
  60.6 0.8 reshape.35
  61.9 3.5 %collective-permute-start.6 = (bf16[16,2,16]{2,0,1:T(8,128)(2,1)S(1)}, bf16[16,2,16]{2,0,1:T(8,128)(2,1)S(1)}, u32[]{:S(2)}, u32[]{:S(2)}) collective-permute-start(bf16[16,2,16]{2,0,1:T(8,128)(2,1)S(1)} %multiply_convert_fusion.1), channel_id=1, source_target_pairs={{0,13},{1,0},{4,1},{5,4},{8,5},{9,8},{12,9},{13,12},{2,15},{3,2},{... | collective-permute-start | bytes 3080 | tf_op jit(solution)/shard_map/ppermute | solution.py:61
  65.4 1.3 collective-permute-done.2
  66.8 3.6 %collective-permute-start.7 = (bf16[16,2,16]{2,0,1:T(8,128)(2,1)S(1)}, bf16[16,2,16]{2,0,1:T(8,128)(2,1)S(1)}, u32[]{:S(2)}, u32[]{:S(2)}) collective-permute-start(bf16[16,2,16]{2,0,1:T(8,128)(2,1)S(1)} %collective-permute-done.6), channel_id=1, source_target_pairs={{0,13},{1,0},{4,1},{5,4},{8,5},{9,8},{12,9},{13,12},{2,15},{3,2},{... | collective-permute-start | bytes 3080 | tf_op jit(solution)/shard_map/ppermute | solution.py:61
  70.3 1.3 collective-permute-done.3
  71.7 3.5 %collective-permute-start.8 = (bf16[16,2,16]{2,0,1:T(8,128)(2,1)S(1)}, bf16[16,2,16]{2,0,1:T(8,128)(2,1)S(1)}, u32[]{:S(2)}, u32[]{:S(2)}) collective-permute-start(bf16[16,2,16]{2,0,1:T(8,128)(2,1)S(1)} %collective-permute-done.7), channel_id=1, source_target_pairs={{0,13},{1,0},{4,1},{5,4},{8,5},{9,8},{12,9},{13,12},{2,15},{3,2},{... | collective-permute-start | bytes 3080 | tf_op jit(solution)/shard_map/ppermute | solution.py:61
  75.2 1.3 collective-permute-done.4
  76.5 2.2 %fusion.82 = (bf16[16,2,64,128]{3,2,1,0:T(8,128)(2,1)}, bf16[16,2,64,128]{3,2,1,0:T(8,128)(2,1)}, bf16[16,2,64,128]{3,2,1,0:T(8,128)(2,1)}, bf16[16,2,64,128]{3,...) fusion(bf16[16,4,64,130]{3,2,1,0:T(8,128)(2,1)S(1)} %fusion.5), kind=kLoop, calls=%fused_computation.108 | loop fusion | bytes 6291456 | tf_op jit(solution)/shard_map/slice | solution.py:29
  78.8 2.6 %collective-permute-done.5 = bf16[16,2,16]{2,0,1:T(8,128)(2,1)S(1)} collective-permute-done((bf16[16,2,16]{2,0,1:T(8,128)(2,1)S(1)}, bf16[16,2,16]{2,0,1:T(8,128)(2,1)S(1)}, u32[]{:S(2)}, u32[]{:S(2)}) %collective-permute-start.5) | collective-permute-done | bytes 1056 | tf_op jit(solution)/shard_map/ppermute | solution.py:59
  81.5 1.4 fusion.16
  83.2 0.3 convolution_bitcast_fusion.4
  83.5 0.3 convolution_bitcast_fusion.7
  84.5 0.3 convolution_bitcast_fusion.6
  85.0 0.3 convolution_bitcast_fusion.9
  85.7 0.7 pad_maximum_fusion.2
  86.4 0.3 convolution_bitcast_fusion.1
  86.7 10.2 %psum.15 = f32[16,32,16]{1,2,0:T(8,128)} all-reduce(f32[16,32,16]{1,2,0:T(8,128)S(1)} %convolution_bitcast_fusion.1), channel_id=1, replica_groups=mesh['groups'=2,'date'=4,'pix'=2,'chan'=2] {'pix'}, use_global_device_ids=true, to_apply=%region_2.3 | all-reduce | flops 8192 | bytes 65536 | tf_op jit(solution)/shard_map/psum | solution.py:85
  96.9 58.0 %all-reduce.3.cloned.1.call-done = f32[3,3,64,32]{2,3,1,0:T(8,128)} async-done(((f32[3,3,64,32]{2,3,1,0:T(8,128)}), f32[3,3,64,32]{2,3,1,0:T(8,128)}) %all-reduce.3.cloned.1.call-update) | async-done | bytes 73744 | tf_op jit(solution)/shard_map/psum | solution.py:86
  154.9 1.6 copy.112
  (62 shorter events, 4.0 us)
Async XLA Ops:
  7.2 20.3 %copy-start = (bf16[16,32,16]{1,2,0:T(8,128)(2,1)S(1)}, bf16[16,32,16]{1,2,0:T(8,128)(2,1)}, u32[]{:S(2)}) copy-start(bf16[16,32,16]{1,2,0:T(8,128)(2,1)} %param.10) | copy-start | bytes 49156
  7.2 15.9 %copy-start.1 = (bf16[16,2,64,128]{3,2,1,0:T(8,128)(2,1)S(1)}, bf16[16,2,64,128]{3,2,1,0:T(8,128)(2,1)}, u32[]{:S(2)}) copy-start(bf16[16,2,64,128]{3,2,1,0:T(8,128)(2,1)} %param.7) | copy-start | bytes 1572868
  7.2 53.4 %reduce-scatter.4.cloned.1.call-start = ((), (), s32[]{:S(2)}) async-start(), calls=%async_computation.2 | async-start | bytes 73728
  8.4 10.4 %collective-permute-start = (bf16[16,1,64,128]{3,2,1,0:T(8,128)(2,1)S(1)}, bf16[16,1,64,128]{3,2,1,0:T(8,128)(2,1)S(1)}, u32[]{:S(2)}, u32[]{:S(2)}) collective-permute-start(bf16[16,1,64,128]{3,2,1,0:T(8,128)(2,1)S(1)} %get-tuple-element.11), channel_id=1, source_target_pairs={{0,2},{1,3},{4,6},{5,7},{8,10},{9,11},{12,14},{13,15},{16,18},{17,... | collective-permute-start | bytes 786440 | tf_op jit(solution)/shard_map/ppermute | solution.py:12
  13.2 10.9 %copy-start.10 = (bf16[3,3,64,32]{2,3,1,0:T(8,128)(2,1)S(1)}, bf16[3,3,64,32]{2,3,1,0:T(8,128)(2,1)}, u32[]{:S(2)}) copy-start(bf16[3,3,64,32]{2,3,1,0:T(8,128)(2,1)} %param.8) | copy-start | bytes 110596
  13.3 9.8 %collective-permute-start.1 = (bf16[16,1,64,128]{3,2,1,0:T(8,128)(2,1)S(1)}, bf16[16,1,64,128]{3,2,1,0:T(8,128)(2,1)S(1)}, u32[]{:S(2)}, u32[]{:S(2)}) collective-permute-start(bf16[16,1,64,128]{3,2,1,0:T(8,128)(2,1)S(1)} %get-tuple-element.12), channel_id=1, source_target_pairs={{2,0},{3,1},{6,4},{7,5},{10,8},{11,9},{14,12},{15,13},{18,16},{19,... | collective-permute-start | bytes 786440 | tf_op jit(solution)/shard_map/ppermute | solution.py:15
  25.3 0.7 copy-start.15
  25.4 0.8 copy-start.2
  26.2 35.3 %copy-start.13 = (f32[16]{0:T(128)S(1)}, f32[16]{0:T(128)}, u32[]{:S(2)}) copy-start(f32[16]{0:T(128)} %param.11) | copy-start | bytes 196
  26.2 35.3 %copy-start.14 = (f32[16]{0:T(128)S(1)}, f32[16]{0:T(128)}, u32[]{:S(2)}) copy-start(f32[16]{0:T(128)} %param.12) | copy-start | bytes 196
  26.2 35.5 %copy-start.11 = (s32[2,16]{1,0:T(2,128)S(1)}, s32[2,16]{1,0:T(2,128)}, u32[]{:S(2)}) copy-start(s32[2,16]{1,0:T(2,128)} %param.13) | copy-start | bytes 388
  30.1 124.8 %all-reduce.3.cloned.1.call-start = ((), (), s32[]{:S(2)}) async-start(), calls=%async_computation.1 | async-start | bytes 294912 | tf_op jit(solution)/shard_map/psum | solution.py:86
  61.7 17.1 %copy-start.12 = (f32[1,2,16]{2,0,1:T(1,128)}, f32[1,2,16]{2,0,1:T(1,128)S(1)}, u32[]{:S(2)}) copy-start(f32[1,2,16]{2,0,1:T(1,128)S(1)} %fusion.28) | copy-start | bytes 388
  61.8 4.9 %collective-permute-start.2 = (bf16[16,2,16]{2,0,1:T(8,128)(2,1)S(1)}, bf16[16,2,16]{2,0,1:T(8,128)(2,1)S(1)}, u32[]{:S(2)}, u32[]{:S(2)}) collective-permute-start(bf16[16,2,16]{2,0,1:T(8,128)(2,1)S(1)} %multiply_convert_fusion.1), channel_id=1, source_target_pairs={{0,1},{1,4},{4,5},{5,8},{8,9},{9,12},{12,13},{13,0},{2,3},{3,6},{6... | collective-permute-start | bytes 3080 | tf_op jit(solution)/shard_map/ppermute | solution.py:59
  61.9 4.9 %collective-permute-start.6 = (bf16[16,2,16]{2,0,1:T(8,128)(2,1)S(1)}, bf16[16,2,16]{2,0,1:T(8,128)(2,1)S(1)}, u32[]{:S(2)}, u32[]{:S(2)}) collective-permute-start(bf16[16,2,16]{2,0,1:T(8,128)(2,1)S(1)} %multiply_convert_fusion.1), channel_id=1, source_target_pairs={{0,13},{1,0},{4,1},{5,4},{8,5},{9,8},{12,9},{13,12},{2,15},{3,2},{... | collective-permute-start | bytes 3080 | tf_op jit(solution)/shard_map/ppermute | solution.py:61
  66.7 4.9 %collective-permute-start.3 = (bf16[16,2,16]{2,0,1:T(8,128)(2,1)S(1)}, bf16[16,2,16]{2,0,1:T(8,128)(2,1)S(1)}, u32[]{:S(2)}, u32[]{:S(2)}) collective-permute-start(bf16[16,2,16]{2,0,1:T(8,128)(2,1)S(1)} %collective-permute-done.2), channel_id=1, source_target_pairs={{0,1},{1,4},{4,5},{5,8},{8,9},{9,12},{12,13},{13,0},{2,3},{3,6},{6... | collective-permute-start | bytes 3080 | tf_op jit(solution)/shard_map/ppermute | solution.py:59
  66.8 4.9 %collective-permute-start.7 = (bf16[16,2,16]{2,0,1:T(8,128)(2,1)S(1)}, bf16[16,2,16]{2,0,1:T(8,128)(2,1)S(1)}, u32[]{:S(2)}, u32[]{:S(2)}) collective-permute-start(bf16[16,2,16]{2,0,1:T(8,128)(2,1)S(1)} %collective-permute-done.6), channel_id=1, source_target_pairs={{0,13},{1,0},{4,1},{5,4},{8,5},{9,8},{12,9},{13,12},{2,15},{3,2},{... | collective-permute-start | bytes 3080 | tf_op jit(solution)/shard_map/ppermute | solution.py:61
  71.6 4.9 %collective-permute-start.4 = (bf16[16,2,16]{2,0,1:T(8,128)(2,1)S(1)}, bf16[16,2,16]{2,0,1:T(8,128)(2,1)S(1)}, u32[]{:S(2)}, u32[]{:S(2)}) collective-permute-start(bf16[16,2,16]{2,0,1:T(8,128)(2,1)S(1)} %collective-permute-done.3), channel_id=1, source_target_pairs={{0,1},{1,4},{4,5},{5,8},{8,9},{9,12},{12,13},{13,0},{2,3},{3,6},{6... | collective-permute-start | bytes 3080 | tf_op jit(solution)/shard_map/ppermute | solution.py:59
  71.7 7.0 %collective-permute-start.8 = (bf16[16,2,16]{2,0,1:T(8,128)(2,1)S(1)}, bf16[16,2,16]{2,0,1:T(8,128)(2,1)S(1)}, u32[]{:S(2)}, u32[]{:S(2)}) collective-permute-start(bf16[16,2,16]{2,0,1:T(8,128)(2,1)S(1)} %collective-permute-done.7), channel_id=1, source_target_pairs={{0,13},{1,0},{4,1},{5,4},{8,5},{9,8},{12,9},{13,12},{2,15},{3,2},{... | collective-permute-start | bytes 3080 | tf_op jit(solution)/shard_map/ppermute | solution.py:61
  76.5 4.9 %collective-permute-start.5 = (bf16[16,2,16]{2,0,1:T(8,128)(2,1)S(1)}, bf16[16,2,16]{2,0,1:T(8,128)(2,1)S(1)}, u32[]{:S(2)}, u32[]{:S(2)}) collective-permute-start(bf16[16,2,16]{2,0,1:T(8,128)(2,1)S(1)} %collective-permute-done.4), channel_id=1, source_target_pairs={{0,1},{1,4},{4,5},{5,8},{8,9},{9,12},{12,13},{13,0},{2,3},{3,6},{6... | collective-permute-start | bytes 3080 | tf_op jit(solution)/shard_map/ppermute | solution.py:59
  78.7 4.2 %copy-start.3 = (bf16[16,2,64,128]{3,2,1,0:T(8,128)(2,1)S(1)}, bf16[16,2,64,128]{3,2,1,0:T(8,128)(2,1)}, u32[]{:S(2)}) copy-start(bf16[16,2,64,128]{3,2,1,0:T(8,128)(2,1)} %copy-done.2) | copy-start | bytes 1572868
  82.9 1.0 copy-start.9
  82.9 1.3 copy-start.8
  83.2 1.3 copy-start.7
  83.5 1.3 copy-start.6
  83.7 1.3 copy-start.5
  84.2 1.2 copy-start.4
Sparse Core Ops, SparseCore 0:
  30.2 30.3 reduce-scatter.3
  86.5 68.3 all-reduce.2
